TPU v7x, 512 devices: a whole 4x4x16 slice. The times are simulated.
512 devices in a mesh: ctx: 64 (over z, x), head: 8 (over y, core).
Axes of the slice: x: 4, y: 4, z: 16, core: 2. Of those that a mesh axis runs over, the one named last changes fastest.
Arguments:
- queries: bfloat16 [8192, 8192], P('ctx', 'head'), may hold values from -6 to 6
- keys: bfloat16 [8192, 8192], P('ctx', 'head'), may hold values from -6 to 6
- values: bfloat16 [8192, 8192], P('ctx', 'head'), may hold values from -6 to 6
- log_decay: float32 [8192, 64], P('ctx', 'head'), may hold values from -1 to 0, as said below
- gain: float32 [8192], P('head'), may hold values from 0.1 to 1.9
- grad_out: bfloat16 [8192, 8192], P('ctx', 'head'), may hold values from -6 to 6
Outputs:
- normed: bfloat16 [8192, 8192], P('ctx', 'head')
- grad_queries: bfloat16 [8192, 8192], P('ctx', 'head')
- grad_keys: bfloat16 [8192, 8192], P('ctx', 'head')
- grad_values: bfloat16 [8192, 8192], P('ctx', 'head')
Inputs may be any that keep to these rules, and one draw needn't show every extreme that they name: `log_decay`: entries are negative.
All inputs are finite; a program needn't handle non-finite values.
Results may differ from a plain program's by a relative error of at most 0.0095.
Values sent between devices are 32-bit elements; how exact they have to be, the bound alone decides.
A program may use at most 128 MiB of HBM per device.

v0:
```python
import jax
import jax.numpy as jnp
from jax import lax
from jax.sharding import Mesh
from jax.sharding import PartitionSpec as P

HEADS = 64
HEAD_DIM = 128
CTX = ("ctx_0", "ctx_1")


epsilon = 1e-06


def filled_with(x, identity):
    return jax.tree.map(
        lambda a, e: jnp.broadcast_to(jnp.asarray(e, a.dtype), a.shape), x, identity
    )


def entering_2(x, axes, combine, identity, reverse):
    before = start = filled_with(x, identity)
    running = x
    for axis in reversed(axes):
        devices, index = (lax.axis_size(axis), lax.axis_index(axis))
        pieces = jax.tree.map(lambda part: lax.all_gather(part, axis), running)
        inside, running = (start, start)
        for k in reversed(range(devices)) if reverse else range(devices):
            passed = k > index if reverse else k < index
            running = combine(running, jax.tree.map(lambda part: part[k], pieces))
            inside = jax.tree.map(lambda new, old: jnp.where(passed, new, old), running, inside)
        before = combine(inside, before)
    return before


def from_everyone(x, axis):
    copies = jnp.broadcast_to(x, (lax.axis_size(axis), *x.shape))
    return lax.all_to_all(copies, axis, split_axis=0, concat_axis=0, tiled=True)


def taken_together(x, axis):
    return from_everyone(x, axis).sum(axis=0)


def together(arrays, axis):
    ends = [0]
    for a in arrays:
        ends.append(ends[-1] + a.size)
    running = taken_together(jnp.concatenate([a.ravel() for a in arrays]), axis)
    return tuple((running[b:e].reshape(a.shape) for a, b, e in zip(arrays, ends, ends[1:])))


def combine_forward(earlier, later):
    return (earlier[0] * later[0], later[0][:, None, None] * earlier[1] + later[1])


def combine_backward(earlier, later):
    return (earlier[0] * later[0], later[1] + later[0][:, None, None] * earlier[1])


def split_pair(array):
    high = array.astype(jnp.bfloat16)
    low = (array - high.astype(jnp.float32)).astype(jnp.bfloat16)
    return (high, low)


def paired_product(form, data, array):
    high, low = split_pair(array)
    return jnp.einsum(form, data, high, preferred_element_type=jnp.float32) + jnp.einsum(
        form, data, low, preferred_element_type=jnp.float32
    )


def body(queries, keys, values, log_decay, gain, grad_out):
    row_count = queries.shape[0]
    head_count = log_decay.shape[1]
    head_width = queries.shape[1] // head_count
    query_heads = queries.reshape(row_count, head_count, head_width)
    key_heads = keys.reshape(row_count, head_count, head_width)
    value_heads = values.reshape(row_count, head_count, head_width)
    cumulative = jnp.cumsum(log_decay, axis=0)
    last_log = cumulative[-1]
    log_rows = cumulative.T
    spread = log_rows[:, :, None] - log_rows[:, None, :]
    token_position = lax.broadcasted_iota(jnp.int32, (row_count, row_count), 0)
    source = lax.broadcasted_iota(jnp.int32, (row_count, row_count), 1)
    decay_matrix = jnp.where(
        (token_position >= source)[None], jnp.exp(jnp.minimum(spread, 0.0)), 0.0
    )
    key_decay = jnp.exp(last_log[None, :] - cumulative)
    key_scaled = (key_decay[:, :, None] * key_heads.astype(jnp.float32)).astype(jnp.bfloat16)
    local_state = jnp.einsum(
        "thd,the->hde", key_scaled, value_heads, preferred_element_type=jnp.float32
    )
    block_decay = jnp.exp(last_log)
    identity = (
        jnp.ones((head_count,), jnp.float32),
        jnp.zeros((head_count, head_width, head_width), jnp.float32),
    )
    entering = entering_2((block_decay, local_state), CTX, combine_forward, identity, False)[1]
    scores = jnp.einsum("thd,shd->hts", query_heads, key_heads, preferred_element_type=jnp.float32)
    weights = (scores * decay_matrix).astype(jnp.bfloat16)
    intra_out = jnp.einsum("hts,shd->thd", weights, value_heads, preferred_element_type=jnp.float32)
    query_decay = jnp.exp(cumulative)
    inter_out = query_decay[:, :, None] * paired_product("thd,hde->the", query_heads, entering)
    attended = (intra_out + inter_out).reshape(row_count, head_count * head_width)
    scaled_grad = grad_out.astype(jnp.float32) * gain[None, :]
    local_squares = jnp.sum(attended * attended, axis=1)
    local_products = jnp.sum(scaled_grad * attended, axis=1)
    total_width = HEADS * HEAD_DIM
    squares, products = together((local_squares, local_products), "head")
    inverse = lax.rsqrt(squares / total_width + epsilon)
    normed = (attended * inverse[:, None] * gain[None, :]).astype(jnp.bfloat16)
    grad_attended = (
        inverse[:, None] * scaled_grad - attended * (inverse**3 * products / total_width)[:, None]
    ).astype(jnp.bfloat16)
    grad_heads = grad_attended.reshape(row_count, head_count, head_width)
    decayed_grad = query_decay[:, :, None] * grad_heads.astype(jnp.float32)
    grad_state = paired_product("thd,the->hde", query_heads, decayed_grad)
    later_grad = entering_2((block_decay, grad_state), CTX, combine_backward, identity, True)[1]
    grad_weights = jnp.einsum(
        "the,she->hts", grad_heads, value_heads, preferred_element_type=jnp.float32
    )
    grad_scores = (grad_weights * decay_matrix).astype(jnp.bfloat16)
    grad_query = jnp.einsum(
        "hts,shd->thd", grad_scores, key_heads, preferred_element_type=jnp.float32
    ) + query_decay[:, :, None] * paired_product("the,hde->thd", grad_heads, entering)
    grad_key = jnp.einsum(
        "hts,thd->shd", grad_scores, query_heads, preferred_element_type=jnp.float32
    ) + key_decay[:, :, None] * paired_product("she,hde->shd", value_heads, later_grad)
    grad_value = jnp.einsum(
        "hts,thd->shd", weights, grad_heads, preferred_element_type=jnp.float32
    ) + paired_product("shd,hde->she", key_scaled, later_grad)
    flat = (row_count, head_count * head_width)
    return (
        normed,
        grad_query.reshape(flat).astype(jnp.bfloat16),
        grad_key.reshape(flat).astype(jnp.bfloat16),
        grad_value.reshape(flat).astype(jnp.bfloat16),
    )


def solution(mesh):
    finer = Mesh(mesh.devices.reshape(16, 4, mesh.shape["head"]), ("ctx_0", "ctx_1", "head"))
    in_specs = (
        P(CTX, "head"),
        P(CTX, "head"),
        P(CTX, "head"),
        P(CTX, "head"),
        P("head"),
        P(CTX, "head"),
    )
    out_specs = (P(CTX, "head"), P(CTX, "head"), P(CTX, "head"), P(CTX, "head"))
    return jax.shard_map(body, mesh=finer, in_specs=in_specs, out_specs=out_specs, check_vma=False)
```

profile of v0, /device:TPU:6, one launch (start us, length us, event | category | flops | bytes accessed | tf_op | source)
XLA Modules:
  0.0 338.9 jit_solution(11531772819006520830)
XLA Ops:
  7.2 0.0 all-gather.14.cloned.1.call-start
  7.2 1.1 copy.116
  8.4 0.8 copy.119
  9.2 0.2 reduce_window_sum.11
  9.4 2.0 fusion.71
  11.5 0.0 all-gather.10.cloned.1.call-start
  11.5 11.6 %all-gather.2 = f32[4,1,8]{2,1,0:T(1,128)S(1)} all-gather(f32[1,1,8]{2,1,0:T(1,128)S(1)} %get-tuple-element.24), channel_id=1, replica_groups=mesh['ctx_0'=16,'ctx_1'=4,'head'=8] {'ctx_1'}, dimensions={0}, use_global_device_ids=true | all-gather | bytes 160 | tf_op jit(solution)/shard_map/all_gather | solution.py:26
  23.1 29.6 %all-gather.14.cloned.1.call-done = f32[32,128,128]{2,1,0:T(8,128)} async-done(((f32[8,128,128]{2,1,0:T(8,128)}), f32[32,128,128]{2,1,0:T(8,128)}) %all-gather.14.cloned.1.call-update) | async-done | bytes 2097168 | tf_op jit(solution)/shard_map/all_gather | solution.py:26
  52.7 2.7 bitcast_add_fusion.1
  55.4 0.0 all-gather.10.cloned.1.call-update
  55.4 0.0 all-gather.16.cloned.1.call-start
  55.5 0.1 copy.120
  55.6 30.0 %all-gather.3 = f32[16,1,8]{2,1,0:T(1,128)S(1)} all-gather(f32[1,1,8]{2,1,0:T(1,128)S(1)} %get-tuple-element.63), channel_id=1, replica_groups=mesh['ctx_0'=16,'ctx_1'=4,'head'=8] {'ctx_0'}, dimensions={0}, use_global_device_ids=true | all-gather | bytes 544 | tf_op jit(solution)/shard_map/all_gather | solution.py:26
  85.6 0.2 fusion.12
  85.9 77.6 %all-gather.10.cloned.1.call-done = f32[16,8,128,128]{3,2,1,0:T(8,128)} async-done(((f32[1,8,128,128]{3,2,1,0:T(8,128)}), f32[16,8,128,128]{3,2,1,0:T(8,128)}) %all-gather.10.cloned.1.call-update) | async-done | bytes 8388624 | tf_op jit(solution)/shard_map/all_gather | solution.py:26
  163.5 4.3 %fusion.38 = f32[8,128,128]{2,1,0:T(8,128)S(1)} fusion(f32[16,8,128,128]{3,2,1,0:T(8,128)} %all-gather.10.cloned.1.call-done, f32[32,128,128]{2,1,0:T(8,128)S(1)} %copy-done.1, f32[8]{0:T(128)S(1)} %get-tuple-element.60, f32[8]{0:T(128)S(1)} %get-tuple-element.67, f32[8]{0:T(128)S(1)} %get-tuple-element.66, f32[8]{0:T(128)S(1)} %get-tuple-element.65, ...), kind=kLoop, calls=%fused_computation.65 | loop fusion | flops 7864320 | bytes 11010740 | tf_op jit(solution)/shard_map/add | solution.py:54
  167.7 0.3 fusion.76
  168.1 0.3 fusion.10
  168.4 0.3 copy-done.3
  168.7 0.3 multiply_reduce_fusion.1
  169.0 0.2 copy.132
  169.3 0.2 multiply_reduce_fusion
  169.4 9.4 %all_to_all.6 = f32[8,1,256]{2,1,0:T(1,128)S(1)} all-to-all(f32[8,1,256]{2,1,0:T(1,128)S(1)} %broadcast_in_dim.13), channel_id=1, replica_groups=mesh['ctx_0'=16,'ctx_1'=4,'head'=8] {'head'}, dimensions={0} | all-to-all | bytes 16384 | tf_op jit(solution)/shard_map/all_to_all | solution.py:38
  178.9 0.9 subtract_convert_fusion.2
  179.8 0.2 copy.134
  179.9 0.2 fusion.64
  180.2 0.2 fusion.6
  180.4 1.0 copy.142
  181.4 0.0 all-gather.12.cloned.1.call-start
  181.5 32.8 %all-gather.16.cloned.1.call-done = f32[32,128,128]{2,1,0:T(8,128)} async-done(((f32[8,128,128]{2,1,0:T(8,128)}), f32[32,128,128]{2,1,0:T(8,128)}) %all-gather.16.cloned.1.call-update) | async-done | bytes 2097168 | tf_op jit(solution)/shard_map/all_gather | solution.py:26
  214.3 2.5 fusion.59
  216.9 30.0 %all-gather.4 = f32[16,1,8]{2,1,0:T(1,128)S(1)} all-gather(f32[1,1,8]{2,1,0:T(1,128)S(1)} %get-tuple-element.62), channel_id=1, replica_groups=mesh['ctx_0'=16,'ctx_1'=4,'head'=8] {'ctx_0'}, dimensions={0}, use_global_device_ids=true | all-gather | bytes 544 | tf_op jit(solution)/shard_map/all_gather | solution.py:26
  246.9 0.3 fusion.13
  247.2 0.2 fusion.104
  247.4 0.2 fusion.8
  247.7 0.3 fusion.15
  248.0 0.9 copy.149
  248.8 2.0 fusion.108
  250.8 74.1 %all-gather.12.cloned.1.call-done = f32[16,8,128,128]{3,2,1,0:T(8,128)} async-done(((f32[1,8,128,128]{3,2,1,0:T(8,128)}), f32[16,8,128,128]{3,2,1,0:T(8,128)}) %all-gather.12.cloned.1.call-update) | async-done | bytes 8388624 | tf_op jit(solution)/shard_map/all_gather | solution.py:26
  324.9 4.2 %fusion.34 = f32[8,128,128]{2,1,0:T(8,128)S(1)} fusion(f32[16,8,128,128]{3,2,1,0:T(8,128)} %all-gather.12.cloned.1.call-done, f32[32,128,128]{2,1,0:T(8,128)S(1)} %copy-done.2, f32[8]{0:T(128)S(1)} %get-tuple-element.41, f32[8]{0:T(128)S(1)} %get-tuple-element.27, f32[8]{0:T(128)S(1)} %get-tuple-element.28, f32[8]{0:T(128)S(1)} %get-tuple-element.29, ...), kind=kLoop, calls=%fused_computation.60 | loop fusion | flops 7864320 | bytes 11010740 | tf_op jit(solution)/shard_map/add | solution.py:58
  329.1 0.3 fusion.68
  329.4 0.3 fusion.82
  329.7 0.3 fusion.5
  330.1 0.0 copy-done.7
  330.1 0.3 fusion.14
  330.4 0.9 copy.150
  331.2 0.3 fusion.11
  331.5 0.9 copy.151
  (37 shorter events, 0.3 us)
Async XLA Ops:
  7.2 78.5 %copy-start = (bf16[128,1024]{1,0:T(8,128)(2,1)S(1)}, bf16[128,1024]{1,0:T(8,128)(2,1)}, u32[]{:S(2)}) copy-start(bf16[128,1024]{1,0:T(8,128)(2,1)} %param.6) | copy-start | bytes 786436
  7.2 45.5 %all-gather.14.cloned.1.call-start = ((), (), s32[]{:S(2)}) async-start(), calls=%async_computation.3 | async-start | bytes 2621440 | tf_op jit(solution)/shard_map/all_gather | solution.py:26
  11.5 152.0 %all-gather.10.cloned.1.call-start = ((), (), s32[]{:S(2)}) async-start(), calls=%async_computation.1 | async-start | bytes 8912896 | tf_op jit(solution)/shard_map/all_gather | solution.py:26
  52.7 110.8 %copy-start.1 = (f32[32,128,128]{2,1,0:T(8,128)S(1)}, f32[32,128,128]{2,1,0:T(8,128)}, u32[]{:S(2)}) copy-start(f32[32,128,128]{2,1,0:T(8,128)} %all-gather.14.cloned.1.call-done) | copy-start | bytes 6291460
  55.4 158.9 %all-gather.16.cloned.1.call-start = ((), (), s32[]{:S(2)}) async-start(), calls=%async_computation.4 | async-start | bytes 2621440 | tf_op jit(solution)/shard_map/all_gather | solution.py:26
  85.9 82.5 %copy-start.9 = (bf16[8,128,128]{2,1,0:T(8,128)(2,1)}, bf16[8,128,128]{2,1,0:T(8,128)(2,1)S(1)}, u32[]{:S(2)}) copy-start(bf16[8,128,128]{2,1,0:T(8,128)(2,1)S(1)} %fusion.12) | copy-start | bytes 786436
  167.7 1.0 copy-start.3
  168.1 1.2 copy-start.8
  168.1 1.2 copy-start.10
  181.4 143.5 %all-gather.12.cloned.1.call-start = ((), (), s32[]{:S(2)}) async-start(), calls=%async_computation.2 | async-start | bytes 8912896 | tf_op jit(solution)/shard_map/all_gather | solution.py:26
  247.2 0.8 copy-start.6
  247.4 77.5 %copy-start.2 = (f32[32,128,128]{2,1,0:T(8,128)S(1)}, f32[32,128,128]{2,1,0:T(8,128)}, u32[]{:S(2)}) copy-start(f32[32,128,128]{2,1,0:T(8,128)} %all-gather.16.cloned.1.call-done) | copy-start | bytes 6291460
  324.9 4.2 %copy-start.4 = (bf16[128,1024]{1,0:T(8,128)(2,1)S(1)}, bf16[128,1024]{1,0:T(8,128)(2,1)}, u32[]{:S(2)}) copy-start(bf16[128,1024]{1,0:T(8,128)(2,1)} %param.8) | copy-start | bytes 786436
  329.1 1.0 copy-start.7
  329.7 1.5 copy-start.5
Sparse Core Ops, SparseCore 0:
  11.6 41.0 all-gather.13
  55.5 107.9 all-gather.9
  181.5 32.6 all-gather.15
  217.0 107.8 all-gather.11
where the time goes:
time: 340 us; the launch traced here: 339 us
  waiting for transfers between devices  214 us (63%)
  blocking collectives  80.9 us (24%)
  other arithmetic  15 us (4%)
  between operations  14.1 us (4%)
  matrix products  8.18 us (2%)
  local copies, waits for them, and re-layouts  6.4 us (2%)
    all_gather x4, waiting for transfers between devices, entering_2(): pieces = jax.tree.map(lambda part: lax.all_gather(part, axis), running)  214 us
    all_gather x3, blocking collectives, entering_2(): pieces = jax.tree.map(lambda part: lax.all_gather(part, axis), running)  71.5 us
    all_to_all x1, blocking collectives, from_everyone(): return lax.all_to_all(copies, axis, split_axis=0, concat_axis=0, tiled=True)  9.4 us
    add x2, other arithmetic, combine_forward(): later[0][:, None, None] * earlier[1] + later[1]  6.95 us
  transfers between devices with their start and end apart: 4, of which 4 were waited for; matrix products, arithmetic and copies ran while one was open for 1% of the time, Pallas kernels for 0%

commit v1 on v0

v1 whole, which is shorter than its diff:
```python
import functools

import jax
import jax.numpy as jnp
from jax import lax
from jax.experimental import pallas as pl
from jax.experimental.pallas import tpu as pltpu
from jax.sharding import Mesh
from jax.sharding import PartitionSpec as P

HEADS = 64
HEAD_DIM = 128
GROUP = 8
GROUPS = 8
PARTS = 2
LOCAL_HEADS = 8
PART_HEADS = LOCAL_HEADS // PARTS
SLICE = HEAD_DIM // GROUP
ROWS = PART_HEADS * SLICE
SUB = ROWS // GROUPS
FAR_FIRST = (4, 3, 5, 2, 6, 1, 7)
AXES = ("zh", "zl", "x", "head")
MESH = pl.DeviceIdType.MESH

epsilon = 1e-06


def dot(a, b, ca, cb, precision=None):
    return lax.dot_general(
        a, b, (((ca,), (cb,)), ((), ())), preferred_element_type=jnp.float32, precision=precision
    )


def kernel(
    q_hbm, k_hbm, v_hbm, log_ref, gain_ref, g_hbm,
    normed_out, gq_out, gk_out, gv_out,
    q_ref, k_ref, v_ref, g_ref, n_ref, gq_ref, gk_ref, gv_ref,
    decay_ref, kd_ref, qd_ref, ks_ref, qst_ref, w_ref, att_ref, sg_ref, ga_ref, s_ref, gki_ref, gvi_ref,
    a_send, a_recv, z_send, z_recv, y_send, y_recv, b_send, b_recv,
    a2_send, a2_recv, z2_send, z2_recv, y2_send, y2_recv, b2_send, b2_recv,
    h_send, h_recv, in_sem, out_sem, send_sem, recv_sem,
):
    zh, zl, x, head = (lax.axis_index(a) for a in AXES)
    me = zl * 4 + x

    def group_device(j):
        return (zh, lax.div(j, 4), lax.rem(j, 4), head)

    def groups_device(j):
        return (j, zl, x, head)

    def head_device(j):
        return (zh, zl, x, j)

    def copies(src, dst, mine, device, slot, arriving):
        for k in FAR_FIRST:
            j = lax.rem(mine + (8 - k if arriving else k), 8)
            yield pltpu.make_async_remote_copy(
                src_ref=src(j),
                dst_ref=dst(j if arriving else mine),
                send_sem=send_sem.at[slot, k - 1],
                recv_sem=recv_sem.at[slot, k - 1],
                device_id=device(j),
                device_id_type=MESH,
            )

    def exchange(src, dst, mine, device, slot):
        for c in copies(src, dst, mine, device, slot, False):
            c.start()

    def arrived(src, dst, mine, device, slot):
        for c in copies(src, dst, mine, device, slot, True):
            c.wait_recv()

    def sent(src, dst, mine, device, slot):
        for c in copies(src, dst, mine, device, slot, False):
            c.wait_send()

    barrier = pltpu.get_barrier_semaphore()
    for mine, device in ((zh, groups_device), (me, group_device), (head, head_device)):
        for k in FAR_FIRST:
            pl.semaphore_signal(
                barrier, inc=1, device_id=device(lax.rem(mine + k, 8)), device_id_type=MESH
            )
    loads = [
        pltpu.make_async_copy(a, b, in_sem.at[i])
        for i, (a, b) in enumerate(((k_hbm, k_ref), (v_hbm, v_ref), (q_hbm, q_ref), (g_hbm, g_ref)))
    ]
    for c in loads:
        c.start()

    def cols(h):
        return slice(h * HEAD_DIM, (h + 1) * HEAD_DIM)

    n = HEAD_DIM
    row = lax.broadcasted_iota(jnp.int32, (n, n), 0)
    col = lax.broadcasted_iota(jnp.int32, (n, n), 1)
    log_rows = jnp.concatenate(
        [log_ref[...], jnp.zeros((n, n - LOCAL_HEADS), jnp.float32)], axis=1
    ).T[:LOCAL_HEADS]
    upto = jnp.where(row <= col, 1.0, 0.0).astype(jnp.float32)
    cum = dot(log_rows, upto, 1, 0, lax.Precision.HIGHEST)
    last = jnp.broadcast_to(cum[:, n - 1 :], (LOCAL_HEADS, n))
    block_decay = jnp.exp(last)

    def across(r):
        return jnp.broadcast_to(r, (n, n))

    def plan(s, r, mine, device, slot):
        return (s, r, mine, device, slot)

    def at(ref, c):
        return lambda j: ref.at[c, j]

    plans = {}
    slot = 0
    for name, (s, r, mine, device) in {
        "a": (a_send, a_recv, me, group_device),
        "z": (z_send, z_recv, zh, groups_device),
        "y": (y_send, y_recv, zh, groups_device),
        "b": (b_send, b_recv, me, group_device),
        "a2": (a2_send, a2_recv, me, group_device),
        "z2": (z2_send, z2_recv, zh, groups_device),
        "y2": (y2_send, y2_recv, zh, groups_device),
        "b2": (b2_send, b2_recv, me, group_device),
    }.items():
        for c in range(PARTS):
            plans[name, c] = (at(s, c), at(r, c), mine, device, slot)
            slot += 1
    plans["h"] = (lambda j: h_send, lambda j: h_recv.at[j], head, head_device, slot)

    def go(name, c, s, r, mine):
        r[c, mine] = s[c, mine]
        exchange(*plans[name, c])

    loads[0].wait()
    loads[1].wait()
    for c in range(PARTS):
        for i in range(PART_HEADS):
            h = c * PART_HEADS + i
            cum_col = across(cum[h : h + 1]).T
            key_decay = jnp.exp(last[h : h + 1] - cum_col)
            kd_ref[h] = key_decay
            qd_ref[h] = jnp.exp(cum_col)
            ks = (key_decay * k_ref[:, cols(h)].astype(jnp.float32)).astype(jnp.bfloat16)
            ks_ref[h] = ks
            decay_ref[h] = jnp.where(
                row >= col, jnp.exp(jnp.minimum(cum_col - across(cum[h : h + 1]), 0.0)), 0.0
            )
            state = dot(ks, v_ref[:, cols(h)], 0, 0)
            a_send[c, :, i * SLICE : (i + 1) * SLICE, :] = state.reshape(GROUP, SLICE, n)
        a_send[c, :, ROWS:, :] = jnp.broadcast_to(block_decay[None], (GROUP, LOCAL_HEADS, n))
        if c == 0:
            pl.semaphore_wait(barrier, 21)
        go("a", c, a_send, a_recv, me)

    loads[2].wait()
    loads[3].wait()

    def forward_local(h):
        q = q_ref[:, cols(h)]
        w = (dot(q, k_ref[:, cols(h)], 1, 1) * decay_ref[h]).astype(jnp.bfloat16)
        w_ref[h] = w
        att_ref[h] = dot(w, v_ref[:, cols(h)], 1, 0)

    def forward_more(h):
        qst_ref[h] = (qd_ref[h] * q_ref[:, cols(h)].astype(jnp.float32)).T.astype(jnp.bfloat16)
        sg_ref[h] = g_ref[:, cols(h)].astype(jnp.float32) * gain_ref[:, cols(h)]

    for h in range(LOCAL_HEADS):
        forward_local(h)

    def decay_of(c, j, i):
        h = c * PART_HEADS + i
        return a_recv[c, j, ROWS + h : ROWS + h + 1, :]

    def part(i):
        return slice(i * SLICE, (i + 1) * SLICE)

    forward = range(8)
    backward = range(7, -1, -1)

    for c in range(PARTS):
        arrived(*plans["a", c])
        folded, decays = [], []
        for i in range(PART_HEADS):
            total = a_recv[c, 0, part(i), :]
            decay = decay_of(c, 0, i)
            for j in range(1, GROUP):
                d = decay_of(c, j, i)
                total = d * total + a_recv[c, j, part(i), :]
                decay = d * decay
            folded.append(total)
            decays.append(jnp.broadcast_to(decay, (SLICE * 8 // SUB, n)))
        z_send[c, :, :SUB, :] = jnp.concatenate(folded, axis=0).reshape(GROUPS, SUB, n)
        z_send[c, :, SUB:, :] = jnp.concatenate(decays, axis=0).reshape(GROUPS, 8, n)
        go("z", c, z_send, z_recv, zh)

    for h in range(LOCAL_HEADS):
        forward_more(h)

    for c in range(PARTS):
        arrived(*plans["z", c])
        state = jnp.zeros((SUB, n), jnp.float32)
        for g in forward:
            y_send[c, g] = state
            state = z_recv[c, g, SUB : SUB + 1, :] * state + z_recv[c, g, :SUB, :]
        go("y", c, y_send, y_recv, zh)

    for c in range(PARTS):
        arrived(*plans["y", c])
        entering = y_recv[c].reshape(ROWS, n)
        for i in range(PART_HEADS):
            state = entering[part(i)]
            for j in forward:
                b_send[c, j, part(i), :] = state
                state = decay_of(c, j, i) * state + a_recv[c, j, part(i), :]
        go("b", c, b_send, b_recv, me)

    squares = jnp.zeros((n, n), jnp.float32)
    products = jnp.zeros((n, n), jnp.float32)
    for c in range(PARTS):
        arrived(*plans["b", c])
        for i in range(PART_HEADS):
            h = c * PART_HEADS + i
            state = b_recv[c, :, part(i), :].reshape(n, n).astype(jnp.bfloat16)
            s_ref[h] = state
            att = att_ref[h] + qd_ref[h] * dot(q_ref[:, cols(h)], state, 1, 0)
            att_ref[h] = att
            squares += att * att
            products += sg_ref[h] * att

    ones = jnp.ones((8, n), jnp.float32)
    sums = jnp.where(
        lax.broadcasted_iota(jnp.int32, (8, n), 0) == 0,
        dot(ones, squares, 1, 1, lax.Precision.HIGHEST),
        dot(ones, products, 1, 1, lax.Precision.HIGHEST),
    )
    h_send[...] = sums
    h_recv[head] = sums
    exchange(*plans["h"])
    arrived(*plans["h"])
    sums = h_recv[0]
    for j in range(1, 8):
        sums += h_recv[j]
    width = HEADS * HEAD_DIM
    inverse_row = lax.rsqrt(sums[0:1] / width + epsilon)
    factor_row = inverse_row * inverse_row * inverse_row * sums[1:2] / width
    inverse = across(inverse_row).T
    factor = across(factor_row).T

    for c in range(PARTS):
        for i in range(PART_HEADS):
            h = c * PART_HEADS + i
            ga = (inverse * sg_ref[h] - att_ref[h] * factor).astype(jnp.bfloat16)
            ga_ref[h] = ga
            a2_send[c, :, part(i), :] = dot(qst_ref[h], ga, 1, 0).reshape(GROUP, SLICE, n)
        go("a2", c, a2_send, a2_recv, me)

    def backward_local(h):
        ga = ga_ref[h]
        gs = (dot(ga, v_ref[:, cols(h)], 1, 1) * decay_ref[h]).astype(jnp.bfloat16)
        gq_ref[:, cols(h)] = (
            dot(gs, k_ref[:, cols(h)], 1, 0) + qd_ref[h] * dot(ga, s_ref[h], 1, 1)
        ).astype(jnp.bfloat16)
        gki_ref[h] = dot(gs, q_ref[:, cols(h)], 0, 0)
        gvi_ref[h] = dot(w_ref[h], ga, 0, 0)
        n_ref[:, cols(h)] = (att_ref[h] * inverse * gain_ref[:, cols(h)]).astype(jnp.bfloat16)

    for h in range(PART_HEADS):
        backward_local(h)

    for c in range(PARTS):
        arrived(*plans["a2", c])
        folded = []
        for i in range(PART_HEADS):
            total = a2_recv[c, GROUP - 1, part(i), :]
            for j in range(GROUP - 2, -1, -1):
                total = decay_of(c, j, i) * total + a2_recv[c, j, part(i), :]
            folded.append(total)
        z2_send[c] = jnp.concatenate(folded, axis=0).reshape(GROUPS, SUB, n)
        go("z2", c, z2_send, z2_recv, zh)

    for h in range(PART_HEADS, LOCAL_HEADS):
        backward_local(h)
    stores = [
        pltpu.make_async_copy(a, b, out_sem.at[i])
        for i, (a, b) in enumerate(
            ((n_ref, normed_out), (gq_ref, gq_out), (gk_ref, gk_out), (gv_ref, gv_out))
        )
    ]
    stores[0].start()
    stores[1].start()

    for c in range(PARTS):
        arrived(*plans["z2", c])
        state = jnp.zeros((SUB, n), jnp.float32)
        for g in backward:
            y2_send[c, g] = state
            state = z_recv[c, g, SUB : SUB + 1, :] * state + z2_recv[c, g]
        go("y2", c, y2_send, y2_recv, zh)

    for c in range(PARTS):
        arrived(*plans["y2", c])
        later = y2_recv[c].reshape(ROWS, n)
        for i in range(PART_HEADS):
            state = later[part(i)]
            for j in backward:
                b2_send[c, j, part(i), :] = state
                state = decay_of(c, j, i) * state + a2_recv[c, j, part(i), :]
        go("b2", c, b2_send, b2_recv, me)

    for key, p in plans.items():
        if key[0] != "b2":
            sent(*p)

    for c in range(PARTS):
        arrived(*plans["b2", c])
        for i in range(PART_HEADS):
            h = c * PART_HEADS + i
            state = b2_recv[c, :, part(i), :].reshape(n, n).astype(jnp.bfloat16)
            gk_ref[:, cols(h)] = (
                gki_ref[h] + kd_ref[h] * dot(v_ref[:, cols(h)], state, 1, 1)
            ).astype(jnp.bfloat16)
            gv_ref[:, cols(h)] = (gvi_ref[h] + dot(ks_ref[h], state, 1, 0)).astype(jnp.bfloat16)
    stores[2].start()
    stores[3].start()
    for c in range(PARTS):
        sent(*plans["b2", c])
    for c in stores:
        c.wait()


def body(queries, keys, values, log_decay, gain, grad_out):
    n = HEAD_DIM
    shape = queries.shape
    f32, bf16 = jnp.float32, jnp.bfloat16
    anywhere = pl.BlockSpec(memory_space=pl.ANY)
    vmem = pl.BlockSpec(memory_space=pltpu.VMEM)
    full = pltpu.VMEM(shape, bf16)
    wide = pltpu.VMEM((LOCAL_HEADS, n, n), f32)
    half = pltpu.VMEM((LOCAL_HEADS, n, n), bf16)

    def slots(rows):
        return [pltpu.VMEM((PARTS, 8, rows, n), f32)] * 2

    return tuple(
        pl.pallas_call(
            kernel,
            out_shape=[jax.ShapeDtypeStruct(shape, bf16)] * 4,
            in_specs=[anywhere, anywhere, anywhere, vmem, vmem, anywhere],
            out_specs=[anywhere] * 4,
            scratch_shapes=[
                *[full] * 8,
                wide, wide, wide, half, half, half, wide, wide, half, half, wide, wide,
                *slots(ROWS + 8), *slots(SUB + 8), *slots(SUB), *slots(ROWS),
                *slots(ROWS), *slots(SUB), *slots(SUB), *slots(ROWS),
                pltpu.VMEM((8, n), f32), pltpu.VMEM((8, 8, n), f32),
                pltpu.SemaphoreType.DMA((4,)), pltpu.SemaphoreType.DMA((4,)),
                pltpu.SemaphoreType.DMA((8 * PARTS + 1, 7)), pltpu.SemaphoreType.DMA((8 * PARTS + 1, 7)),
            ],
            compiler_params=pltpu.CompilerParams(
                collective_id=0, has_side_effects=True, vmem_limit_bytes=40 * 2**20
            ),
            cost_estimate=pl.CostEstimate(flops=600_000_000, bytes_accessed=3_000_000, transcendentals=400_000),
        )(queries, keys, values, log_decay, gain.reshape(1, -1), grad_out)
    )


def solution(mesh):
    finer = Mesh(mesh.devices.reshape(8, 2, 4, mesh.shape["head"]), AXES)
    ctx = ("zh", "zl", "x")
    both = P(ctx, "head")
    return jax.shard_map(
        body,
        mesh=finer,
        in_specs=(both, both, both, both, P("head"), both),
        out_specs=(both,) * 4,
        check_vma=False,
    )
```

time: 340 us -> 93.7 us (0.28)
  waiting for transfers between devices: 214 us -> 0 us
  Pallas kernels: 0 us -> 85.3 us
  blocking collectives: 80.9 us -> 0 us
  other arithmetic: 15 us -> 0 us
  between operations: 14.1 us -> 0.66 us
  matrix products: 8.18 us -> 0 us
    all_gather x4 -> x0, waiting for transfers between devices: 214 us -> none  [entering_2(): pieces = jax.tree.map(lambda part: lax.all_gather(part, axis), running)]
    pallas_call x0 -> x1, Pallas kernels: none -> 85.3 us  [body(): pl.pallas_call(kernel, out_shape=[jax.ShapeDtypeStruct(shape, bf16)] * 4,...]
    all_gather x3 -> x0, blocking collectives: 71.5 us -> none  [entering_2(): pieces = jax.tree.map(lambda part: lax.all_gather(part, axis), running)]
    add x4 -> x0, other arithmetic: 13.7 us -> none  [the longest x2 6.95 us: combine_forward(): later[0][:, None, None] * earlier[1] + later[1]]
    all_to_all x1 -> x0, blocking collectives: 9.4 us -> none  [from_everyone(): return lax.all_to_all(copies, axis, split_axis=0, concat_axis=0, tiled=True)]
    dot_general x17 -> x0, matrix products: 8.18 us -> none  [the longest x1 2 us: body(): jnp.einsum('thd,the->hde', key_scaled, value_heads, preferred_element_typ...]
    unnamed x28 -> x15, local copies, waits for them, and re-layouts: 4.85 us -> 7.4 us
  transfers between devices with their start and end apart: 4 -> 0, of which waited for: 4 -> 0; matrix products, arithmetic and copies ran while one was open for 1% -> 0% of each run, Pallas kernels for 0% -> 0%
where the time goes in v1:
time: 93.7 us; the launch traced here: 93.4 us
  Pallas kernels  85.3 us (91%)
  local copies, waits for them, and re-layouts  7.4 us (8%)
    pallas_call x1, Pallas kernels, body(): pl.pallas_call(kernel, out_shape=[jax.ShapeDtypeStruct(shape, bf16)] * 4,...  85.3 us
    unnamed x15, local copies, waits for them, and re-layouts  7.4 us

profile of v1, /device:TPU:6, one launch (start us, length us, event | category | flops | bytes accessed | tf_op | source)
XLA Modules:
  0.0 93.4 jit_solution(9130724949979952333)
XLA Ops:
  0.6 0.0 copy-start.4
  0.6 0.8 copy.10.log_ref
  1.4 0.0 copy-done.4
  1.4 0.0 copy-start
  1.5 0.9 %copy-done = bf16[128,1024]{1,0:T(8,128)(2,1)S(1)} copy-done((bf16[128,1024]{1,0:T(8,128)(2,1)S(1)}, bf16[128,1024]{1,0:T(8,128)(2,1)}, u32[]{:S(2)}) %copy-start) | copy-done | bytes 262168
  2.4 0.0 copy-start.1
  2.4 0.9 %copy-done.1 = bf16[128,1024]{1,0:T(8,128)(2,1)S(1)} copy-done((bf16[128,1024]{1,0:T(8,128)(2,1)S(1)}, bf16[128,1024]{1,0:T(8,128)(2,1)}, u32[]{:S(2)}) %copy-start.1) | copy-done | bytes 262168
  3.3 0.0 copy-start.2
  3.3 0.9 %copy-done.2 = bf16[128,1024]{1,0:T(8,128)(2,1)S(1)} copy-done((bf16[128,1024]{1,0:T(8,128)(2,1)S(1)}, bf16[128,1024]{1,0:T(8,128)(2,1)}, u32[]{:S(2)}) %copy-start.2) | copy-done | bytes 262168
  4.3 0.0 copy-start.3
  4.3 0.9 %copy-done.3 = bf16[128,1024]{1,0:T(8,128)(2,1)S(1)} copy-done((bf16[128,1024]{1,0:T(8,128)(2,1)S(1)}, bf16[128,1024]{1,0:T(8,128)(2,1)}, u32[]{:S(2)}) %copy-start.3) | copy-done | bytes 262168
  5.2 85.3 %shard_map.93 = (bf16[128,1024]{1,0:T(8,128)(2,1)S(1)}, bf16[128,1024]{1,0:T(8,128)(2,1)S(1)}, bf16[128,1024]{1,0:T(8,128)(2,1)S(1)}, bf16[128,1024]{1,0:T(8,128)(2,1)S(1)}) custom-call(bf16[128,1024]{1,0:T(8,128)(2,1)S(1)} %copy-done, bf16[128,1024]{1,0:T(8,128)(2,1)S(1)} %copy-done.1, bf16[128,1024]{1,0:T(8,128)(2,1)S(1)} %copy-done.2, ...), custom_call_target="tpu_custom_call" | custom-call | flops 600000000 | bytes 3000000 | tf_op jit(solution)/shard_map/pallas_call | solution.py:348
  90.6 0.7 copy.15
  91.3 0.7 copy.16
  92.0 0.7 copy.17
  92.7 0.7 copy.18
Async XLA Ops:
  0.6 0.8 copy-start.4
  1.4 1.0 %copy-start = (bf16[128,1024]{1,0:T(8,128)(2,1)S(1)}, bf16[128,1024]{1,0:T(8,128)(2,1)}, u32[]{:S(2)}) copy-start(bf16[128,1024]{1,0:T(8,128)(2,1)} %q_hbm.1) | copy-start | bytes 786436
  2.4 0.9 %copy-start.1 = (bf16[128,1024]{1,0:T(8,128)(2,1)S(1)}, bf16[128,1024]{1,0:T(8,128)(2,1)}, u32[]{:S(2)}) copy-start(bf16[128,1024]{1,0:T(8,128)(2,1)} %k_hbm.1) | copy-start | bytes 786436
  3.3 0.9 %copy-start.2 = (bf16[128,1024]{1,0:T(8,128)(2,1)S(1)}, bf16[128,1024]{1,0:T(8,128)(2,1)}, u32[]{:S(2)}) copy-start(bf16[128,1024]{1,0:T(8,128)(2,1)} %v_hbm.1) | copy-start | bytes 786436
  4.3 0.9 %copy-start.3 = (bf16[128,1024]{1,0:T(8,128)(2,1)S(1)}, bf16[128,1024]{1,0:T(8,128)(2,1)}, u32[]{:S(2)}) copy-start(bf16[128,1024]{1,0:T(8,128)(2,1)} %g_hbm.1) | copy-start | bytes 786436

commit v2 on v1

--- a/solution.py
+++ b/solution.py
@@ -17,6 +17,7 @@
 PART_HEADS = LOCAL_HEADS // PARTS
 SLICE = HEAD_DIM // GROUP
 ROWS = PART_HEADS * SLICE
+VMEM_LIMIT = 56 * 2**20
 SUB = ROWS // GROUPS
 FAR_FIRST = (4, 3, 5, 2, 6, 1, 7)
 AXES = ("zh", "zl", "x", "head")
@@ -38,7 +39,7 @@
     decay_ref, kd_ref, qd_ref, ks_ref, qst_ref, w_ref, att_ref, sg_ref, ga_ref, s_ref, gki_ref, gvi_ref,
     a_send, a_recv, z_send, z_recv, y_send, y_recv, b_send, b_recv,
     a2_send, a2_recv, z2_send, z2_recv, y2_send, y2_recv, b2_send, b2_recv,
-    h_send, h_recv, in_sem, out_sem, send_sem, recv_sem,
+    h_send, h_recv, in_sem, out_sem, send_sem, recv_sem, near_sem, far_sem,
 ):
     zh, zl, x, head = (lax.axis_index(a) for a in AXES)
     me = zl * 4 + x
@@ -77,11 +78,15 @@
             c.wait_send()
 
     barrier = pltpu.get_barrier_semaphore()
-    for mine, device in ((zh, groups_device), (me, group_device), (head, head_device)):
-        for k in FAR_FIRST:
+    def tell(sem, mine, device, offsets):
+        for k in offsets:
             pl.semaphore_signal(
-                barrier, inc=1, device_id=device(lax.rem(mine + k, 8)), device_id_type=MESH
+                sem, inc=1, device_id=device(lax.rem(mine + k, 8)), device_id_type=MESH
             )
+
+    tell(barrier, me, group_device, FAR_FIRST)
+    tell(barrier, head, head_device, FAR_FIRST)
+    tell(barrier, zh, groups_device, (1, 7))
     loads = [
         pltpu.make_async_copy(a, b, in_sem.at[i])
         for i, (a, b) in enumerate(((k_hbm, k_ref), (v_hbm, v_ref), (q_hbm, q_ref), (g_hbm, g_ref)))
@@ -95,19 +100,13 @@
     n = HEAD_DIM
     row = lax.broadcasted_iota(jnp.int32, (n, n), 0)
     col = lax.broadcasted_iota(jnp.int32, (n, n), 1)
-    log_rows = jnp.concatenate(
-        [log_ref[...], jnp.zeros((n, n - LOCAL_HEADS), jnp.float32)], axis=1
-    ).T[:LOCAL_HEADS]
     upto = jnp.where(row <= col, 1.0, 0.0).astype(jnp.float32)
-    cum = dot(log_rows, upto, 1, 0, lax.Precision.HIGHEST)
+    cum = dot(log_ref[...], upto, 1, 0, lax.Precision.HIGHEST)
     last = jnp.broadcast_to(cum[:, n - 1 :], (LOCAL_HEADS, n))
     block_decay = jnp.exp(last)
 
     def across(r):
         return jnp.broadcast_to(r, (n, n))
-
-    def plan(s, r, mine, device, slot):
-        return (s, r, mine, device, slot)
 
     def at(ref, c):
         return lambda j: ref.at[c, j]
@@ -151,9 +150,12 @@
             a_send[c, :, i * SLICE : (i + 1) * SLICE, :] = state.reshape(GROUP, SLICE, n)
         a_send[c, :, ROWS:, :] = jnp.broadcast_to(block_decay[None], (GROUP, LOCAL_HEADS, n))
         if c == 0:
-            pl.semaphore_wait(barrier, 21)
+            pl.semaphore_wait(barrier, 16)
+            tell(near_sem, zh, groups_device, (1, 7))
         go("a", c, a_send, a_recv, me)
 
+    pl.semaphore_wait(near_sem, 2)
+    tell(far_sem, zh, groups_device, (2, 6))
     loads[2].wait()
     loads[3].wait()
 
@@ -180,6 +182,7 @@
     forward = range(8)
     backward = range(7, -1, -1)
 
+    pl.semaphore_wait(far_sem, 2)
     for c in range(PARTS):
         arrived(*plans["a", c])
         folded, decays = [], []
@@ -230,11 +233,10 @@
             squares += att * att
             products += sg_ref[h] * att
 
-    ones = jnp.ones((8, n), jnp.float32)
     sums = jnp.where(
         lax.broadcasted_iota(jnp.int32, (8, n), 0) == 0,
-        dot(ones, squares, 1, 1, lax.Precision.HIGHEST),
-        dot(ones, products, 1, 1, lax.Precision.HIGHEST),
+        jnp.sum(squares.T, axis=0, keepdims=True),
+        jnp.sum(products.T, axis=0, keepdims=True),
     )
     h_send[...] = sums
     h_recv[head] = sums
@@ -331,11 +333,24 @@
         c.wait()
 
 
+def write_out(*refs):
+    held, load_sem, store_sem = refs[8:]
+    loads = [pltpu.make_async_copy(refs[i], held.at[i], load_sem.at[i]) for i in range(4)]
+    stores = [pltpu.make_async_copy(held.at[i], refs[4 + i], store_sem.at[i]) for i in range(4)]
+    for c in loads:
+        c.start()
+    for load, store in zip(loads, stores):
+        load.wait()
+        store.start()
+    for c in stores:
+        c.wait()
+
+
 def body(queries, keys, values, log_decay, gain, grad_out):
     n = HEAD_DIM
     shape = queries.shape
     f32, bf16 = jnp.float32, jnp.bfloat16
-    anywhere = pl.BlockSpec(memory_space=pl.ANY)
+    hbm = pl.BlockSpec(memory_space=pltpu.HBM)
     vmem = pl.BlockSpec(memory_space=pltpu.VMEM)
     full = pltpu.VMEM(shape, bf16)
     wide = pltpu.VMEM((LOCAL_HEADS, n, n), f32)
@@ -344,12 +359,11 @@
     def slots(rows):
         return [pltpu.VMEM((PARTS, 8, rows, n), f32)] * 2
 
-    return tuple(
-        pl.pallas_call(
+    made = pl.pallas_call(
             kernel,
             out_shape=[jax.ShapeDtypeStruct(shape, bf16)] * 4,
-            in_specs=[anywhere, anywhere, anywhere, vmem, vmem, anywhere],
-            out_specs=[anywhere] * 4,
+            in_specs=[hbm, hbm, hbm, vmem, vmem, hbm],
+            out_specs=[hbm] * 4,
             scratch_shapes=[
                 *[full] * 8,
                 wide, wide, wide, half, half, half, wide, wide, half, half, wide, wide,
@@ -358,12 +372,26 @@
                 pltpu.VMEM((8, n), f32), pltpu.VMEM((8, 8, n), f32),
                 pltpu.SemaphoreType.DMA((4,)), pltpu.SemaphoreType.DMA((4,)),
                 pltpu.SemaphoreType.DMA((8 * PARTS + 1, 7)), pltpu.SemaphoreType.DMA((8 * PARTS + 1, 7)),
+                pltpu.SemaphoreType.REGULAR, pltpu.SemaphoreType.REGULAR,
             ],
             compiler_params=pltpu.CompilerParams(
-                collective_id=0, has_side_effects=True, vmem_limit_bytes=40 * 2**20
+                collective_id=0, has_side_effects=True, vmem_limit_bytes=VMEM_LIMIT
             ),
             cost_estimate=pl.CostEstimate(flops=600_000_000, bytes_accessed=3_000_000, transcendentals=400_000),
-        )(queries, keys, values, log_decay, gain.reshape(1, -1), grad_out)
+        )(queries, keys, values, log_decay.T, gain.reshape(1, -1), grad_out)
+    return tuple(
+        pl.pallas_call(
+            write_out,
+            out_shape=[jax.ShapeDtypeStruct(shape, bf16)] * 4,
+            in_specs=[hbm] * 4,
+            out_specs=[hbm] * 4,
+            scratch_shapes=[
+                pltpu.VMEM((4, *shape), bf16),
+                pltpu.SemaphoreType.DMA((4,)),
+                pltpu.SemaphoreType.DMA((4,)),
+            ],
+            compiler_params=pltpu.CompilerParams(vmem_limit_bytes=VMEM_LIMIT),
+        )(*made)
     )
 
 

time: 93.7 us -> 83.6 us (0.89)
  local copies, waits for them, and re-layouts: 7.4 us -> 0 us
  Pallas kernels: 85.3 us -> 82.5 us
    unnamed x15 -> x0, local copies, waits for them, and re-layouts: 7.4 us -> none
    pallas_call x1, Pallas kernels: 85.3 us -> 80.5 us  [body(): pl.pallas_call(kernel, out_shape=[jax.ShapeDtypeStruct(shape, bf16)] * 4,...]
    pallas_call x0 -> x1, Pallas kernels: none -> 1.98 us  [body(): pl.pallas_call(write_out, out_shape=[jax.ShapeDtypeStruct(shape, bf16)] *...]
where the time goes in v2:
time: 83.6 us; the launch traced here: 83.1 us
  Pallas kernels  82.5 us (99%)
    pallas_call x1, Pallas kernels, body(): pl.pallas_call(kernel, out_shape=[jax.ShapeDtypeStruct(shape, bf16)] * 4,...  80.5 us
    pallas_call x1, Pallas kernels, body(): pl.pallas_call(write_out, out_shape=[jax.ShapeDtypeStruct(shape, bf16)] *...  1.98 us

profile of v2, /device:TPU:6, one launch (start us, length us, event | category | flops | bytes accessed | tf_op | source)
XLA Modules:
  0.0 83.1 jit_solution(6822765058061895893)
XLA Ops:
  0.6 80.5 %shard_map.93 = (bf16[128,1024]{1,0:T(8,128)(2,1)}, bf16[128,1024]{1,0:T(8,128)(2,1)}, bf16[128,1024]{1,0:T(8,128)(2,1)}, bf16[128,1024]{1,0:T(8,128)(2,1)}) custom-call(bf16[128,1024]{1,0:T(8,128)(2,1)} %q_hbm.1, bf16[128,1024]{1,0:T(8,128)(2,1)} %k_hbm.1, bf16[128,1024]{1,0:T(8,128)(2,1)} %v_hbm.1, f32[8,128]{1,0:T(8,128)} %bitcast.2, f32[1,1024]{1,0:T(1,128)} %bitcast.3, ...), custom_call_target="tpu_custom_call" | custom-call | flops 600000000 | bytes 3000000 | tf_op jit(solution)/shard_map/pallas_call | solution.py:362
  81.2 2.0 %shard_map.94 = (bf16[128,1024]{1,0:T(8,128)(2,1)}, bf16[128,1024]{1,0:T(8,128)(2,1)}, bf16[128,1024]{1,0:T(8,128)(2,1)}, bf16[128,1024]{1,0:T(8,128)(2,1)}) custom-call(bf16[128,1024]{1,0:T(8,128)(2,1)} %get-tuple-element.8.refs_0_, bf16[128,1024]{1,0:T(8,128)(2,1)} %get-tuple-element.9.refs_1_, bf16[128,1024]{1,0:T(8,128)(2,1)} %get-tuple-element.10.refs_2_, ...), custom_call_target="tpu_custom_call" | custom-call | tf_op jit(solution)/shard_map/pallas_call | solution.py:383

commit v3 on v2

--- a/solution.py
+++ b/solution.py
@@ -17,7 +17,7 @@
 PART_HEADS = LOCAL_HEADS // PARTS
 SLICE = HEAD_DIM // GROUP
 ROWS = PART_HEADS * SLICE
-VMEM_LIMIT = 56 * 2**20
+VMEM_LIMIT = 54016 * 1024
 SUB = ROWS // GROUPS
 FAR_FIRST = (4, 3, 5, 2, 6, 1, 7)
 AXES = ("zh", "zl", "x", "head")
@@ -34,12 +34,12 @@
 
 def kernel(
     q_hbm, k_hbm, v_hbm, log_ref, gain_ref, g_hbm,
-    normed_out, gq_out, gk_out, gv_out,
-    q_ref, k_ref, v_ref, g_ref, n_ref, gq_ref, gk_ref, gv_ref,
-    decay_ref, kd_ref, qd_ref, ks_ref, qst_ref, w_ref, att_ref, sg_ref, ga_ref, s_ref, gki_ref, gvi_ref,
+    n_ref, gq_ref, gk_ref, gv_ref,
+    q_ref, k_ref, v_ref, g_ref,
+    cum_ref, decay_ref, kd_ref, qd_ref, ks_ref, qst_ref, w_ref, att_ref, sg_ref, ga_ref, s_ref, gki_ref, gvi_ref,
     a_send, a_recv, z_send, z_recv, y_send, y_recv, b_send, b_recv,
     a2_send, a2_recv, z2_send, z2_recv, y2_send, y2_recv, b2_send, b2_recv,
-    h_send, h_recv, in_sem, out_sem, send_sem, recv_sem, near_sem, far_sem,
+    h_send, h_recv, in_sem, send_sem, recv_sem, near_sem, far_sem,
 ):
     zh, zl, x, head = (lax.axis_index(a) for a in AXES)
     me = zl * 4 + x
@@ -140,12 +140,9 @@
             cum_col = across(cum[h : h + 1]).T
             key_decay = jnp.exp(last[h : h + 1] - cum_col)
             kd_ref[h] = key_decay
-            qd_ref[h] = jnp.exp(cum_col)
+            cum_ref[h] = cum_col
             ks = (key_decay * k_ref[:, cols(h)].astype(jnp.float32)).astype(jnp.bfloat16)
             ks_ref[h] = ks
-            decay_ref[h] = jnp.where(
-                row >= col, jnp.exp(jnp.minimum(cum_col - across(cum[h : h + 1]), 0.0)), 0.0
-            )
             state = dot(ks, v_ref[:, cols(h)], 0, 0)
             a_send[c, :, i * SLICE : (i + 1) * SLICE, :] = state.reshape(GROUP, SLICE, n)
         a_send[c, :, ROWS:, :] = jnp.broadcast_to(block_decay[None], (GROUP, LOCAL_HEADS, n))
@@ -161,6 +158,11 @@
 
     def forward_local(h):
         q = q_ref[:, cols(h)]
+        cum_col = cum_ref[h]
+        qd_ref[h] = jnp.exp(cum_col)
+        decay_ref[h] = jnp.where(
+            row >= col, jnp.exp(jnp.minimum(cum_col - across(cum[h : h + 1]), 0.0)), 0.0
+        )
         w = (dot(q, k_ref[:, cols(h)], 1, 1) * decay_ref[h]).astype(jnp.bfloat16)
         w_ref[h] = w
         att_ref[h] = dot(w, v_ref[:, cols(h)], 1, 0)
@@ -285,15 +287,6 @@
 
     for h in range(PART_HEADS, LOCAL_HEADS):
         backward_local(h)
-    stores = [
-        pltpu.make_async_copy(a, b, out_sem.at[i])
-        for i, (a, b) in enumerate(
-            ((n_ref, normed_out), (gq_ref, gq_out), (gk_ref, gk_out), (gv_ref, gv_out))
-        )
-    ]
-    stores[0].start()
-    stores[1].start()
-
     for c in range(PARTS):
         arrived(*plans["z2", c])
         state = jnp.zeros((SUB, n), jnp.float32)
@@ -325,23 +318,15 @@
                 gki_ref[h] + kd_ref[h] * dot(v_ref[:, cols(h)], state, 1, 1)
             ).astype(jnp.bfloat16)
             gv_ref[:, cols(h)] = (gvi_ref[h] + dot(ks_ref[h], state, 1, 0)).astype(jnp.bfloat16)
-    stores[2].start()
-    stores[3].start()
     for c in range(PARTS):
         sent(*plans["b2", c])
+
+
+def write_out(*refs):
+    sem = refs[8]
+    stores = [pltpu.make_async_copy(refs[i], refs[4 + i], sem.at[i]) for i in range(4)]
     for c in stores:
-        c.wait()
-
-
-def write_out(*refs):
-    held, load_sem, store_sem = refs[8:]
-    loads = [pltpu.make_async_copy(refs[i], held.at[i], load_sem.at[i]) for i in range(4)]
-    stores = [pltpu.make_async_copy(held.at[i], refs[4 + i], store_sem.at[i]) for i in range(4)]
-    for c in loads:
         c.start()
-    for load, store in zip(loads, stores):
-        load.wait()
-        store.start()
     for c in stores:
         c.wait()
 
@@ -363,14 +348,14 @@
             kernel,
             out_shape=[jax.ShapeDtypeStruct(shape, bf16)] * 4,
             in_specs=[hbm, hbm, hbm, vmem, vmem, hbm],
-            out_specs=[hbm] * 4,
+            out_specs=[vmem] * 4,
             scratch_shapes=[
-                *[full] * 8,
-                wide, wide, wide, half, half, half, wide, wide, half, half, wide, wide,
+                *[full] * 4,
+                wide, wide, wide, wide, half, half, half, wide, wide, half, half, wide, wide,
                 *slots(ROWS + 8), *slots(SUB + 8), *slots(SUB), *slots(ROWS),
                 *slots(ROWS), *slots(SUB), *slots(SUB), *slots(ROWS),
                 pltpu.VMEM((8, n), f32), pltpu.VMEM((8, 8, n), f32),
-                pltpu.SemaphoreType.DMA((4,)), pltpu.SemaphoreType.DMA((4,)),
+                pltpu.SemaphoreType.DMA((4,)),
                 pltpu.SemaphoreType.DMA((8 * PARTS + 1, 7)), pltpu.SemaphoreType.DMA((8 * PARTS + 1, 7)),
                 pltpu.SemaphoreType.REGULAR, pltpu.SemaphoreType.REGULAR,
             ],
@@ -383,14 +368,10 @@
         pl.pallas_call(
             write_out,
             out_shape=[jax.ShapeDtypeStruct(shape, bf16)] * 4,
-            in_specs=[hbm] * 4,
+            in_specs=[pl.BlockSpec(memory_space=pl.ANY)] * 4,
             out_specs=[hbm] * 4,
-            scratch_shapes=[
-                pltpu.VMEM((4, *shape), bf16),
-                pltpu.SemaphoreType.DMA((4,)),
-                pltpu.SemaphoreType.DMA((4,)),
-            ],
-            compiler_params=pltpu.CompilerParams(vmem_limit_bytes=VMEM_LIMIT),
+            scratch_shapes=[pltpu.SemaphoreType.DMA((4,))],
+            compiler_params=pltpu.CompilerParams(vmem_limit_bytes=16 * 2**20),
         )(*made)
     )
 

time: 83.6 us -> 82.7 us (0.989)
  Pallas kernels: 82.5 us -> 80.1 us
  local copies, waits for them, and re-layouts: 0 us -> 1.37 us
    pallas_call x1, Pallas kernels: 80.5 us -> 79.1 us  [body(): pl.pallas_call(kernel, out_shape=[jax.ShapeDtypeStruct(shape, bf16)] * 4,...]
    unnamed x0 -> x4, local copies, waits for them, and re-layouts: none -> 1.37 us
    pallas_call x1, Pallas kernels: 1.98 us -> 1 us  [body(): pl.pallas_call(write_out, out_shape=[jax.ShapeDtypeStruct(shape, bf16)] *...]
where the time goes in v3:
time: 82.7 us; the launch traced here: 82.2 us
  Pallas kernels  80.1 us (97%)
  local copies, waits for them, and re-layouts  1.37 us (2%)
    pallas_call x1, Pallas kernels, body(): pl.pallas_call(kernel, out_shape=[jax.ShapeDtypeStruct(shape, bf16)] * 4,...  79.1 us

profile of v3, /device:TPU:6, one launch (start us, length us, event | category | flops | bytes accessed | tf_op | source)
XLA Modules:
  0.0 82.2 jit_solution(18176070249270533626)
XLA Ops:
  0.6 0.0 copy-start
  0.6 0.7 copy-done
  1.3 0.0 copy-start.1
  1.3 0.7 copy-done.1
  2.0 79.1 %shard_map.93 = (bf16[128,1024]{1,0:T(8,128)(2,1)S(1)}, bf16[128,1024]{1,0:T(8,128)(2,1)S(1)}, bf16[128,1024]{1,0:T(8,128)(2,1)S(1)}, bf16[128,1024]{1,0:T(8,128)(2,1)S(1)}) custom-call(bf16[128,1024]{1,0:T(8,128)(2,1)} %q_hbm.1, bf16[128,1024]{1,0:T(8,128)(2,1)} %k_hbm.1, bf16[128,1024]{1,0:T(8,128)(2,1)} %v_hbm.1, f32[8,128]{1,0:T(8,128)S(1)} %bitcast.2, ...), custom_call_target="tpu_custom_call" | custom-call | flops 600000000 | bytes 3000000 | tf_op jit(solution)/shard_map/pallas_call | solution.py:347
  81.2 1.0 %shard_map.94 = (bf16[128,1024]{1,0:T(8,128)(2,1)}, bf16[128,1024]{1,0:T(8,128)(2,1)}, bf16[128,1024]{1,0:T(8,128)(2,1)}, bf16[128,1024]{1,0:T(8,128)(2,1)}) custom-call(bf16[128,1024]{1,0:T(8,128)(2,1)S(1)} %get-tuple-element.8.refs_0_, bf16[128,1024]{1,0:T(8,128)(2,1)S(1)} %get-tuple-element.9.refs_1_, bf16[128,1024]{1,0:T(8,128)(2,1)S(1)} %get-tuple-element.10.refs_2_, ...), custom_call_target="tpu_custom_call" | custom-call | tf_op jit(solution)/shard_map/pallas_call | solution.py:368
Async XLA Ops:
  0.6 0.7 copy-start
  1.3 0.7 copy-start.1

commit v4 on v3

--- a/solution.py
+++ b/solution.py
@@ -20,6 +20,7 @@
 VMEM_LIMIT = 54016 * 1024
 SUB = ROWS // GROUPS
 FAR_FIRST = (4, 3, 5, 2, 6, 1, 7)
+GROUP_FAR_FIRST = (6, 2, 5, 3, 7, 1, 4)
 AXES = ("zh", "zl", "x", "head")
 MESH = pl.DeviceIdType.MESH
 
@@ -54,7 +55,7 @@
         return (zh, zl, x, j)
 
     def copies(src, dst, mine, device, slot, arriving):
-        for k in FAR_FIRST:
+        for k in GROUP_FAR_FIRST if device is group_device else FAR_FIRST:
             j = lax.rem(mine + (8 - k if arriving else k), 8)
             yield pltpu.make_async_remote_copy(
                 src_ref=src(j),

time: 82.7 us -> 81 us (0.979)
  Pallas kernels: 80.1 us -> 78.7 us
    pallas_call x1, Pallas kernels: 79.1 us -> 77.8 us  [body(): pl.pallas_call(kernel, out_shape=[jax.ShapeDtypeStruct(shape, bf16)] * 4,...]
where the time goes in v4:
time: 81 us; the launch traced here: 80.8 us
  Pallas kernels  78.7 us (97%)
  local copies, waits for them, and re-layouts  1.37 us (2%)
    pallas_call x1, Pallas kernels, body(): pl.pallas_call(kernel, out_shape=[jax.ShapeDtypeStruct(shape, bf16)] * 4,...  77.8 us

profile of v4, /device:TPU:6, one launch (start us, length us, event | category | flops | bytes accessed | tf_op | source)
XLA Modules:
  0.0 80.8 jit_solution(17993045955003761634)
XLA Ops:
  0.6 0.0 copy-start
  0.6 0.7 copy-done
  1.3 0.0 copy-start.1
  1.3 0.7 copy-done.1
  2.0 77.8 %shard_map.93 = (bf16[128,1024]{1,0:T(8,128)(2,1)S(1)}, bf16[128,1024]{1,0:T(8,128)(2,1)S(1)}, bf16[128,1024]{1,0:T(8,128)(2,1)S(1)}, bf16[128,1024]{1,0:T(8,128)(2,1)S(1)}) custom-call(bf16[128,1024]{1,0:T(8,128)(2,1)} %q_hbm.1, bf16[128,1024]{1,0:T(8,128)(2,1)} %k_hbm.1, bf16[128,1024]{1,0:T(8,128)(2,1)} %v_hbm.1, f32[8,128]{1,0:T(8,128)S(1)} %bitcast.2, ...), custom_call_target="tpu_custom_call" | custom-call | flops 600000000 | bytes 3000000 | tf_op jit(solution)/shard_map/pallas_call | solution.py:348
  79.8 1.0 %shard_map.94 = (bf16[128,1024]{1,0:T(8,128)(2,1)}, bf16[128,1024]{1,0:T(8,128)(2,1)}, bf16[128,1024]{1,0:T(8,128)(2,1)}, bf16[128,1024]{1,0:T(8,128)(2,1)}) custom-call(bf16[128,1024]{1,0:T(8,128)(2,1)S(1)} %get-tuple-element.8.refs_0_, bf16[128,1024]{1,0:T(8,128)(2,1)S(1)} %get-tuple-element.9.refs_1_, bf16[128,1024]{1,0:T(8,128)(2,1)S(1)} %get-tuple-element.10.refs_2_, ...), custom_call_target="tpu_custom_call" | custom-call | tf_op jit(solution)/shard_map/pallas_call | solution.py:369
Async XLA Ops:
  0.6 0.7 copy-start
  1.3 0.7 copy-start.1

commit v5 on v4

--- a/solution.py
+++ b/solution.py
@@ -12,7 +12,7 @@
 HEAD_DIM = 128
 GROUP = 8
 GROUPS = 8
-PARTS = 2
+PARTS = 1
 LOCAL_HEADS = 8
 PART_HEADS = LOCAL_HEADS // PARTS
 SLICE = HEAD_DIM // GROUP

time: 81 us -> 79.4 us (0.980)
  Pallas kernels: 78.7 us -> 76.6 us
    pallas_call x1, Pallas kernels: 77.8 us -> 75.6 us  [body(): pl.pallas_call(kernel, out_shape=[jax.ShapeDtypeStruct(shape, bf16)] * 4,...]
where the time goes in v5:
time: 79.4 us; the launch traced here: 78.6 us
  Pallas kernels  76.6 us (96%)
  local copies, waits for them, and re-layouts  1.37 us (2%)
    pallas_call x1, Pallas kernels, body(): pl.pallas_call(kernel, out_shape=[jax.ShapeDtypeStruct(shape, bf16)] * 4,...  75.6 us

profile of v5, /device:TPU:6, one launch (start us, length us, event | category | flops | bytes accessed | tf_op | source)
XLA Modules:
  0.0 78.6 jit_solution(3299266231080401145)
XLA Ops:
  0.6 0.0 copy-start
  0.6 0.7 copy-done
  1.3 0.0 copy-start.1
  1.3 0.7 copy-done.1
  2.0 75.6 %shard_map.93 = (bf16[128,1024]{1,0:T(8,128)(2,1)S(1)}, bf16[128,1024]{1,0:T(8,128)(2,1)S(1)}, bf16[128,1024]{1,0:T(8,128)(2,1)S(1)}, bf16[128,1024]{1,0:T(8,128)(2,1)S(1)}) custom-call(bf16[128,1024]{1,0:T(8,128)(2,1)} %q_hbm.1, bf16[128,1024]{1,0:T(8,128)(2,1)} %k_hbm.1, bf16[128,1024]{1,0:T(8,128)(2,1)} %v_hbm.1, f32[8,128]{1,0:T(8,128)S(1)} %bitcast.2, ...), custom_call_target="tpu_custom_call" | custom-call | flops 600000000 | bytes 3000000 | tf_op jit(solution)/shard_map/pallas_call | solution.py:348
  77.6 1.0 %shard_map.94 = (bf16[128,1024]{1,0:T(8,128)(2,1)}, bf16[128,1024]{1,0:T(8,128)(2,1)}, bf16[128,1024]{1,0:T(8,128)(2,1)}, bf16[128,1024]{1,0:T(8,128)(2,1)}) custom-call(bf16[128,1024]{1,0:T(8,128)(2,1)S(1)} %get-tuple-element.8.refs_0_, bf16[128,1024]{1,0:T(8,128)(2,1)S(1)} %get-tuple-element.9.refs_1_, bf16[128,1024]{1,0:T(8,128)(2,1)S(1)} %get-tuple-element.10.refs_2_, ...), custom_call_target="tpu_custom_call" | custom-call | tf_op jit(solution)/shard_map/pallas_call | solution.py:369
Async XLA Ops:
  0.6 0.7 copy-start
  1.3 0.7 copy-start.1
